TPU v7x, 128 devices: a whole 4x4x4 slice. The times are simulated.
128 devices in a mesh: req: 16 (over y, x), tp: 8 (over z, core).
Axes of the slice: x: 4, y: 4, z: 4, core: 2. Of those that a mesh axis runs over, the one named last changes fastest.
Arguments:
- queries: bfloat16 [256, 8192], P('req', 'tp'), may hold values from -192 to 192
- fresh_key_value: bfloat16 [256, 8, 256], P('req', 'tp'), may hold values from -8 to 8
- key_value_pool: bfloat16 [512, 256, 8, 256], P('req', None, 'tp'), may hold values from -8 to 8
- request_page_table: int32 [256, 4], P('req'), may hold values from 0 to 63, as said below
- cached_length: int32 [256], P('req'), may hold values from 1 to 1024, as said below
- move_holder_shard: int32 [512, 1], P('req'), may hold values from 0 to 15; in each aligned block of 32 rows (0 to 31, 32 to 63, ...) at most 4 rows name the same one
- move_page_index: int32 [512], P('req'), may hold values from 0 to 31
- request_adapter: int32 [256], P('req'), may hold values from 0 to 63
- adapter_storage_slot: int32 [64], replicated, may hold values from 0 to 63, each once
- output_projection: bfloat16 [8192, 8192], P('tp'), may hold values from -0.0625 to 0.0625
- adapter_down_panels: bfloat16 [64, 8192, 64], P('req', 'tp'), may hold values from -0.0625 to 0.0625
- adapter_up_panels: bfloat16 [64, 64, 8192], P('req', None, 'tp'), may hold values from -0.75 to 0.75
Outputs:
- layer_out: bfloat16 [256, 8192], P('req', 'tp')
Inputs may be any that keep to these rules, and one draw needn't show every extreme that they name: `move_holder_shard`: in each aligned block of 32 moves (those of one shard) no holder appears more than 4 times; some holder appears exactly 4 times in some blocks. `request_page_table`: within each block of 16 requests the 64 entries are all different, so each entry of a shard's extended page list serves exactly one page of one request. `cached_length`: each block of 16 requests holds one request of 1024 tokens.
All inputs are finite; a program needn't handle non-finite values.
Results may differ from a plain program's by a relative error of at most 0.0095.
Values may be sent and summed in bfloat16 or wider, within the bound.
A program may use at most 128 MiB of HBM per device.

v0:
```python
import math

import jax
import jax.numpy as jnp
from jax import lax
from jax.sharding import PartitionSpec as P

CAP = 4


MASKED = -1e30


def page_partials(query_head_rows, page_rows, live_counts):
    head_size_value = query_head_rows.shape[-1]
    key_part = page_rows[..., :head_size_value]
    value_part = page_rows[..., head_size_value:]
    scores = jnp.einsum(
        "bkgd,bjtkd->bkgjt", query_head_rows, key_part, preferred_element_type=jnp.float32
    ) / math.sqrt(head_size_value)
    places = jnp.arange(page_rows.shape[2], dtype=jnp.int32)
    in_range = places[None, None, None, None, :] < live_counts[:, None, None, :, None]
    page_max = jnp.max(jnp.where(in_range, scores, MASKED), axis=-1)
    weights = jnp.where(in_range, jnp.exp(scores - page_max[..., None]), 0.0).astype(jnp.bfloat16)
    page_sum = jnp.sum(weights.astype(jnp.float32), axis=-1)
    page_out = jnp.einsum(
        "bkgjt,bjtkd->bkgjd", weights, value_part, preferred_element_type=jnp.float32
    )
    return (page_max, page_sum, page_out)


def merge_pages(page_max, page_sum, page_out, fresh_token_score, own_value):
    overall_max = jnp.maximum(jnp.max(page_max, axis=-1), fresh_token_score)
    rescale = jnp.exp(page_max - overall_max[..., None])
    own_weight = jnp.exp(fresh_token_score - overall_max)
    numerator = (
        jnp.sum(rescale[..., None] * page_out, axis=3)
        + own_weight[..., None] * own_value[:, :, None, :]
    )
    denominator = jnp.sum(rescale * page_sum, axis=-1) + own_weight
    return numerator / denominator[..., None]


def move_slots(holders, shards, capacity):
    onehot = (holders[:, None] == jnp.arange(shards, dtype=jnp.int32)[None, :]).astype(jnp.int32)
    before = jnp.cumsum(onehot, axis=0) - onehot
    arrival_rank = jnp.sum(before * onehot, axis=1)
    return holders * capacity + arrival_rank


def local(
    queries,
    fresh_key_value,
    key_value_pool,
    request_page_table,
    cached_length,
    move_holder_shard,
    move_page_index,
    request_adapter,
    adapter_storage_slot,
    output_projection,
    adapter_down_panels,
    adapter_up_panels,
):
    requests = queries.shape[0]
    kv_local = key_value_pool.shape[2]
    head_size_value = fresh_key_value.shape[2] // 2
    per_group = queries.shape[1] // (kv_local * head_size_value)
    page_len = key_value_pool.shape[1]
    max_pages = request_page_table.shape[1]
    shards = lax.axis_size("req")
    query_head_rows = queries.reshape(requests, kv_local, per_group, head_size_value)
    page_starts = jnp.arange(max_pages, dtype=jnp.int32) * page_len
    live_counts = jnp.clip(cached_length[:, None] - page_starts[None, :], 0, page_len)
    buffer_slot = move_slots(move_holder_shard[:, 0], shards, CAP)
    wanted = (
        jnp.zeros((shards * CAP,), jnp.int32)
        .at[buffer_slot]
        .set(move_page_index)
        .reshape(shards, CAP)
    )
    asked_for = lax.all_to_all(wanted, "req", split_axis=0, concat_axis=0, tiled=True)
    sent_pages = key_value_pool[asked_for]
    arrived = lax.all_to_all(sent_pages, "req", split_axis=0, concat_axis=0, tiled=True)
    moved_pages = arrived.reshape((shards * CAP,) + key_value_pool.shape[1:])[buffer_slot]
    extended = jnp.concatenate([key_value_pool, moved_pages], axis=0)
    page_max, page_sum, page_out = page_partials(
        query_head_rows, extended[request_page_table], live_counts
    )
    fresh_token_score = jnp.einsum(
        "jypf,jyf->jyp",
        query_head_rows,
        fresh_key_value[..., :head_size_value],
        preferred_element_type=jnp.float32,
    ) / math.sqrt(head_size_value)
    own_value = fresh_key_value[..., head_size_value:].astype(jnp.float32)
    attended = merge_pages(page_max, page_sum, page_out, fresh_token_score, own_value)
    attended = attended.reshape(requests, kv_local * per_group * head_size_value).astype(
        jnp.bfloat16
    )
    projected = jnp.dot(attended, output_projection, preferred_element_type=jnp.float32)
    slot_count = adapter_storage_slot.shape[0]
    slot_match = request_adapter[:, None] == jnp.arange(slot_count, dtype=jnp.int32)[None, :]
    request_slot = jnp.sum(jnp.where(slot_match, adapter_storage_slot[None, :], 0), axis=1)
    owner_partials = adapter_down_panels.shape[0]
    owner = request_slot // owner_partials
    in_owner = request_slot % owner_partials
    to_owner = owner[None, :] == jnp.arange(shards, dtype=jnp.int32)[:, None]
    rows_send = jnp.where(to_owner[:, :, None], attended[None], jnp.zeros((), jnp.bfloat16))
    pick_send = (
        to_owner[:, :, None]
        & (in_owner[None, :, None] == jnp.arange(owner_partials, dtype=jnp.int32)[None, None, :])
    ).astype(jnp.bfloat16)
    request_row_block = lax.all_to_all(rows_send, "req", split_axis=0, concat_axis=0, tiled=True)
    pick_block = lax.all_to_all(pick_send, "req", split_axis=0, concat_axis=0, tiled=True)
    down_projected_all = jnp.einsum(
        "kjq,fqx->kjfx", request_row_block, adapter_down_panels, preferred_element_type=jnp.float32
    )
    partial_low = jnp.sum(down_projected_all * pick_block[..., None].astype(jnp.float32), axis=2)
    whole_low = lax.psum(partial_low, "tp").astype(jnp.bfloat16)
    selected_rows = whole_low[:, :, None, :] * pick_block[..., None]
    correction_rows = jnp.einsum(
        "erzh,zhx->erx", selected_rows, adapter_up_panels, preferred_element_type=jnp.float32
    )
    returned = lax.all_to_all(correction_rows, "req", split_axis=0, concat_axis=0, tiled=True)
    adapter_term = jnp.sum(returned, axis=0)
    projected_cols = lax.psum_scatter(projected, "tp", scatter_dimension=1, tiled=True)
    return (projected_cols + adapter_term).astype(jnp.bfloat16)


def solution(mesh):
    return jax.shard_map(
        local,
        mesh=mesh,
        in_specs=(
            P("req", "tp"),
            P("req", "tp", None),
            P("req", None, "tp", None),
            P("req", None),
            P("req"),
            P("req", None),
            P("req"),
            P("req"),
            P(),
            P("tp", None),
            P("req", "tp", None),
            P("req", None, "tp"),
        ),
        out_specs=P("req", "tp"),
        check_vma=False,
    )
```

profile of v0, /device:TPU:1, one launch (start us, length us, event | category | flops | bytes accessed | tf_op | source)
XLA Modules:
  0.0 262.7 jit_solution(12295193764782104284)
XLA Ops:
  6.5 0.8 fusion.15
  7.4 0.8 select_reduce_fusion.2
  8.2 0.7 fusion.18
  8.9 0.8 scatter_custom_fusion
  9.7 0.7 all_to_all.20
  10.4 7.6 %all-to-all-start = ((s32[16,1,4]{2,1,0:T(1,128)}), s32[16,1,4]{2,1,0:T(1,128)S(1)}, u32[]{:S(2)}, u32[]{:S(2)}) async-start(s32[16,1,4]{2,1,0:T(1,128)} %bitcast.4), calls=%async_computation | async-start | bytes 16384 | tf_op jit(solution)/shard_map/all_to_all | solution.py:82
  18.0 0.9 select_reduce_fusion.3
  18.9 0.6 and_convert_fusion
  19.5 4.9 %all-to-all-done = s32[16,1,4]{2,1,0:T(1,128)S(1)} async-done(((s32[16,1,4]{2,1,0:T(1,128)}), s32[16,1,4]{2,1,0:T(1,128)S(1)}, u32[]{:S(2)}, u32[]{:S(2)}) %all-to-all-start) | async-done | bytes 288 | tf_op jit(solution)/shard_map/all_to_all | solution.py:82
  24.4 3.5 %all-to-all-start.3 = ((bf16[16,16,4]{1,2,0:T(4,128)(2,1)}), bf16[16,16,4]{1,2,0:T(4,128)(2,1)S(1)}, u32[]{:S(2)}, u32[]{:S(2)}) async-start(bf16[16,16,4]{1,2,0:T(4,128)(2,1)} %and_convert_fusion), calls=%async_computation.4 | async-start | bytes 32768 | tf_op jit(solution)/shard_map/all_to_all | solution.py:115
  28.1 0.1 reshape.278
  28.2 7.7 %gather_fusion = bf16[64,256,256]{2,1,0:T(8,128)(2,1)} fusion(bf16[32,256,256]{2,1,0:T(8,128)(2,1)} %bitcast.87, s32[1024]{0:T(1024)S(1)} %pad_clamp_fusion.2), kind=kCustom, calls=%fused_computation | custom fusion | bytes 16777472 | tf_op jit(solution)/shard_map/gather | solution.py:83
  35.9 6.6 %all-to-all-start.1 = ((bf16[16,4,256,1,256]{4,2,1,3,0:T(8,128)(2,1)}), bf16[16,4,256,1,256]{4,2,1,3,0:T(8,128)(2,1)}, u32[]{:S(2)}, u32[]{:S(2)}) async-start(bf16[16,4,256,1,256]{4,2,1,3,0:T(8,128)(2,1)} %bitcast.88), calls=%async_computation.1 | async-start | bytes 16777216 | tf_op jit(solution)/shard_map/all_to_all | solution.py:84
  42.6 0.1 reshape.298
  43.1 0.1 fusion.16
  43.2 119.6 %all-to-all-done.1 = bf16[16,4,256,1,256]{4,2,1,3,0:T(8,128)(2,1)} async-done(((bf16[16,4,256,1,256]{4,2,1,3,0:T(8,128)(2,1)}), bf16[16,4,256,1,256]{4,2,1,3,0:T(8,128)(2,1)}, u32[]{:S(2)}, u32[]{:S(2)}) %all-to-all-start.1) | async-done | bytes 8388640 | tf_op jit(solution)/shard_map/all_to_all | solution.py:84
  162.8 6.2 %gather_fusion.1 = bf16[32,256,256]{2,1,0:T(8,128)(2,1)} fusion(bf16[64,256,256]{2,1,0:T(8,128)(2,1)} %bitcast.7, s32[1024]{0:T(1024)S(1)} %pad_clamp_fusion.1), kind=kCustom, calls=%fused_computation.1 | custom fusion | bytes 8388736 | tf_op jit(solution)/shard_map/gather | solution.py:85
  169.0 7.4 %maximum_bitcast_fusion = bf16[64,256,256]{2,1,0:T(8,128)(2,1)} fusion(bf16[32,256,1,256]{3,1,2,0:T(8,128)(2,1)} %bitcast.89, bf16[32,256,1,256]{3,1,2,0:T(8,128)(2,1)} %param.14), kind=kLoop, calls=%fused_computation.4 | loop fusion | flops 4194304 | bytes 16777216 | tf_op jit(solution)/shard_map/concatenate | solution.py:86
  176.4 8.9 %gather_fusion.2 = bf16[64,256,256]{2,1,0:T(8,128)(2,1)} fusion(bf16[64,256,256]{2,1,0:T(8,128)(2,1)} %maximum_bitcast_fusion, s32[1024]{0:T(1024)S(1)} %pad_clamp_fusion), kind=kCustom, calls=%fused_computation.2 | custom fusion | bytes 16777472 | tf_op jit(solution)/shard_map/gather | solution.py:88
  185.3 3.5 %select_reduce_fusion.1 = (f32[16,8,4]{1,2,0:T(4,128)S(1)}, f32[16,8,4,256]{3,1,2,0:T(8,128)S(1)}) fusion(pred[16,4,256]{2,1,0:T(4,128)(4,1)S(1)} %iota_compare_fusion, bf16[16,8,128,1]{2,1,0,3:T(8,128)(2,1)S(1)} %bitcast.99, bf16[16,4,256,1,256]{4,2,1,0,3:T(8,128)(2,1)} %bitcast.90), kind=kOutput, calls=%fused_computation.24 | convolution fusion | flops 33947136 | bytes 4769792 | tf_op jit(solution)/shard_map/bkgd,bjtkd->bkgjt/dot_general | solution.py:18
  188.8 0.3 convert_reduce_fusion
  189.2 2.9 %fusion.7 = f32[16,8,128]{2,1,0:T(8,128)S(1)} fusion(bf16[16,4,256,1,256]{4,2,1,0,3:T(8,128)(2,1)} %bitcast.91, f32[16,8,4]{1,2,0:T(4,128)S(1)} %get-tuple-element.10, f32[16,8,4,256]{3,1,2,0:T(8,128)S(1)} %get-tuple-element.16, f32[16,8,4]{1,2,0:T(4,128)S(1)} %get-tuple-element.15, pred[16,4,256]{2,1,0:T(4,128)(4,1)S(1)} %iota_compare_fusion), kind=kOutput, calls=%fused_computation.16 | convolution fusion | flops 34062336 | bytes 4804608 | tf_op jit(solution)/shard_map/bkgjt,bjtkd->bkgjd/dot_general | solution.py:26
  192.1 0.1 divide_convert_fusion
  192.2 0.9 broadcast_select_fusion
  193.1 4.5 %all-to-all-start.2 = ((bf16[16,16,1024]{2,1,0:T(8,128)(2,1)}), bf16[16,16,1024]{2,1,0:T(8,128)(2,1)S(1)}, u32[]{:S(2)}, u32[]{:S(2)}) async-start(bf16[16,16,1024]{2,1,0:T(8,128)(2,1)} %broadcast_select_fusion), calls=%async_computation.3 | async-start | bytes 1048576 | tf_op jit(solution)/shard_map/all_to_all | solution.py:114
  197.8 8.9 %fusion.22 = f32[16,8192]{1,0:T(8,128)} fusion(bf16[1024,8192]{1,0:T(8,128)(2,1)} %param.21, bf16[2,8,8,128]{3,2,1,0:T(8,128)(2,1)S(1)} %bitcast.93), kind=kOutput, calls=%fused_computation.67 | convolution fusion | flops 268435456 | bytes 17334272 | tf_op jit(solution)/shard_map/dot_general | solution.py:101
  206.7 0.2 all-to-all-done.2
  206.9 0.5 fusion.4
  207.4 27.7 %psum.7 = bf16[16,16,64]{2,1,0:T(8,128)(2,1)S(1)} all-reduce(f32[16,16,64]{2,1,0:T(8,128)S(1)} %fusion.4), channel_id=1, replica_groups=mesh['req'=16,'tp'=8] {'tp'}, use_global_device_ids=true, to_apply=%region_11.12 | all-reduce | flops 16384 | bytes 98304 | tf_op jit(solution)/shard_map/psum | solution.py:120
  235.1 0.5 convolution_bitcast_fusion
  235.5 18.7 %all_to_all.32 = f32[16,16,1024]{2,1,0:T(8,128)S(1)} all-to-all(f32[16,16,1024]{2,1,0:T(8,128)S(1)} %convolution_bitcast_fusion), channel_id=1, replica_groups=mesh['req'=16,'tp'=8] {'req'}, dimensions={0} | all-to-all | bytes 2097152 | tf_op jit(solution)/shard_map/all_to_all | solution.py:125
  254.4 1.5 add_convert_fusion
  (40 shorter events, 0.9 us)
Async XLA Ops:
  6.5 228.5 %copy-start = (bf16[4,64,1024]{2,1,0:T(8,128)(2,1)S(1)}, bf16[4,64,1024]{2,1,0:T(8,128)(2,1)}, u32[]{:S(2)}) copy-start(bf16[4,64,1024]{2,1,0:T(8,128)(2,1)} %param.23) | copy-start | bytes 1572868
  10.4 14.0 %all-to-all-start = ((s32[16,1,4]{2,1,0:T(1,128)}), s32[16,1,4]{2,1,0:T(1,128)S(1)}, u32[]{:S(2)}, u32[]{:S(2)}) async-start(s32[16,1,4]{2,1,0:T(1,128)} %bitcast.4), calls=%async_computation | async-start | bytes 16384 | tf_op jit(solution)/shard_map/all_to_all | solution.py:82
  24.4 11.5 %all-to-all-start.3 = ((bf16[16,16,4]{1,2,0:T(4,128)(2,1)}), bf16[16,16,4]{1,2,0:T(4,128)(2,1)S(1)}, u32[]{:S(2)}, u32[]{:S(2)}) async-start(bf16[16,16,4]{1,2,0:T(4,128)(2,1)} %and_convert_fusion), calls=%async_computation.4 | async-start | bytes 32768 | tf_op jit(solution)/shard_map/all_to_all | solution.py:115
  35.9 6.7 %copy-start.3 = (s32[16,4]{0,1:T(4,128)S(1)}, s32[16,4]{0,1:T(4,128)}, u32[]{:S(2)}) copy-start(s32[16,4]{0,1:T(4,128)} %param.15) | copy-start | bytes 772
  35.9 6.9 %copy-start.4 = (s32[16]{0:T(128)S(1)}, s32[16]{0:T(128)}, u32[]{:S(2)}) copy-start(s32[16]{0:T(128)} %param.16) | copy-start | bytes 196
  35.9 7.0 %copy-start.1 = (bf16[16,1024]{1,0:T(8,128)(2,1)S(1)}, bf16[16,1024]{1,0:T(8,128)(2,1)}, u32[]{:S(2)}) copy-start(bf16[16,1024]{1,0:T(8,128)(2,1)} %param.12) | copy-start | bytes 98308
  35.9 7.1 %copy-start.2 = (bf16[16,1,256]{2,0,1:T(8,128)(2,1)S(1)}, bf16[16,1,256]{2,0,1:T(8,128)(2,1)}, u32[]{:S(2)}) copy-start(bf16[16,1,256]{2,0,1:T(8,128)(2,1)} %param.13) | copy-start | bytes 24580
  35.9 126.9 %all-to-all-start.1 = ((bf16[16,4,256,1,256]{4,2,1,3,0:T(8,128)(2,1)}), bf16[16,4,256,1,256]{4,2,1,3,0:T(8,128)(2,1)}, u32[]{:S(2)}, u32[]{:S(2)}) async-start(bf16[16,4,256,1,256]{4,2,1,3,0:T(8,128)(2,1)} %bitcast.88), calls=%async_computation.1 | async-start | bytes 16777216 | tf_op jit(solution)/shard_map/all_to_all | solution.py:84
  193.1 13.8 %all-to-all-start.2 = ((bf16[16,16,1024]{2,1,0:T(8,128)(2,1)}), bf16[16,16,1024]{2,1,0:T(8,128)(2,1)S(1)}, u32[]{:S(2)}, u32[]{:S(2)}) async-start(bf16[16,16,1024]{2,1,0:T(8,128)(2,1)} %broadcast_select_fusion), calls=%async_computation.3 | async-start | bytes 1048576 | tf_op jit(solution)/shard_map/all_to_all | solution.py:114
  197.7 9.2 %copy-start.5 = (bf16[4,1024,64]{1,2,0:T(8,128)(2,1)S(1)}, bf16[4,1024,64]{1,2,0:T(8,128)(2,1)}, u32[]{:S(2)}) copy-start(bf16[4,1024,64]{1,2,0:T(8,128)(2,1)} %param.22) | copy-start | bytes 1572868
  197.7 56.6 %reduce-scatter.2.cloned.1.call-start = ((), (), s32[]{:S(2)}) async-start(), calls=%async_computation.6 | async-start | bytes 589824 | tf_op jit(solution)/shard_map/reduce_scatter | solution.py:127
Sparse Core Ops, SparseCore 0:
  206.8 33.8 reduce-scatter.1
where the time goes:
time: 267 us; the launch traced here: 263 us
  waiting for transfers between devices  125 us (47%)
  blocking collectives  46.4 us (17%)
  local copies, waits for them, and re-layouts  24.8 us (9%)
  starting transfers between devices  22.3 us (8%)
  matrix products  16.3 us (6%)
  other arithmetic  14.4 us (5%)
  between operations  13.7 us (5%)
    all_to_all x1, waiting for transfers between devices, local(): lax.all_to_all(sent_pages, 'req', split_axis=0, concat_axis=0, tiled=True)  120 us
    psum x1, blocking collectives, local(): whole_low = lax.psum(partial_low, 'tp').astype(jnp.bfloat16)  27.7 us
    all_to_all x1, blocking collectives, local(): lax.all_to_all(correction_rows, 'req', split_axis=0, concat_axis=0, tiled...  18.7 us
    dot_general x1, matrix products, local(): jnp.dot(attended, output_projection, preferred_element_type=jnp.float32)  8.9 us
    gather x1, local copies, waits for them, and re-layouts, local(): extended[request_page_table]  8.9 us
    gather x1, local copies, waits for them, and re-layouts, local(): sent_pages = key_value_pool[asked_for]  7.71 us
    all_to_all x1, starting transfers between devices, local(): lax.all_to_all(wanted, 'req', split_axis=0, concat_axis=0, tiled=True)  7.58 us
    concatenate x1, other arithmetic, local(): extended = jnp.concatenate([key_value_pool, moved_pages], axis=0)  7.41 us
  transfers between devices with their start and end apart: 5, of which 3 were waited for; matrix products, arithmetic and copies ran while one was open for 8% of the time, Pallas kernels for 0%

commit v1 on v0

v1 whole, which is shorter than its diff:
```python
import functools
import math

import jax
import jax.numpy as jnp
from jax import lax
from jax.experimental import pallas as pl
from jax.experimental.pallas import tpu as pltpu
from jax.sharding import PartitionSpec as P

CAP = 4
MASKED = -1e30
F32 = jnp.float32
BF16 = jnp.bfloat16
META = 16


def iota(shape, dim):
    return lax.broadcasted_iota(jnp.int32, shape, dim)


def matmul(a, b):
    return lax.dot_general(a, b, (((1,), (0,)), ((), ())), preferred_element_type=F32)


def matmul_t(a, b):
    return lax.dot_general(a, b, (((1,), (1,)), ((), ())), preferred_element_type=F32)


def as_column(row):
    n = row.shape[1]
    return jnp.sum(jnp.where(iota((n, n), 0) == iota((n, n), 1), row, 0.0), axis=1, keepdims=True)


def as_row(column):
    n = column.shape[0]
    return jnp.sum(jnp.where(iota((n, n), 0) == iota((n, n), 1), column, 0.0), axis=0, keepdims=True)


def page_partial(q, page, live, head):
    scores = matmul_t(q, page[:, :head]) * (1.0 / math.sqrt(head))
    there = iota(scores.shape, 1) < live
    top = jnp.max(jnp.where(there, scores, MASKED), axis=1, keepdims=True)
    weights = jnp.where(there, jnp.exp(scores - top), 0.0).astype(BF16)
    total = jnp.sum(weights.astype(F32), axis=1, keepdims=True)
    return top, total, matmul(weights, page[:, head:])


def kernel(
    shards, tps,
    table, length, holder, index, adapter, storage, q, fresh, pool, w, down, up,
    out,
    pool_v, w_v, down_v, up_v, qmsg, qgot, rmsg, rgot, pick_v, pick_s, info_v, info_s,
    qown, qrh, own_live, fresh_v, o_u, m_u, l_u, att_f, att_b, att_all, psend, pgot,
    lsend, lgot, low_v, bsend, bgot,
    load_sem, w_sem, small_sem, q_sent, q_came, r_sent, r_came, a_sent, a_came,
    p_sent, p_came, l_sent, l_came, b_sent, b_came,
):
    me, tp = lax.axis_index("req"), lax.axis_index("tp")
    reqs, width = q.shape
    head = fresh.shape[1] // 2
    heads = width // head
    pages, page_len, _ = pool.shape
    moves = holder.shape[1]
    page_slots = table.shape[0]
    panels = storage.shape[1] // shards
    rank = down.shape[0] // panels
    columns = out.shape[1]
    qrows = CAP * heads

    pool_copy = pltpu.make_async_copy(pool, pool_v, load_sem.at[0])
    pool_copy.start()
    down_copy = pltpu.make_async_copy(down, down_v, load_sem.at[1])
    up_copy = pltpu.make_async_copy(up, up_v, load_sem.at[2])
    down_copy.start()
    up_copy.start()

    barrier = pltpu.get_barrier_semaphore()

    @pl.loop(1, shards)
    def _(off):
        pl.semaphore_signal(barrier, inc=1, device_id=(lax.rem(me + off, shards), tp), device_id_type=pl.DeviceIdType.MESH)

    @pl.loop(1, tps)
    def _(off):
        pl.semaphore_signal(barrier, inc=1, device_id=(me, lax.rem(tp + off, tps)), device_id_type=pl.DeviceIdType.MESH)

    def to_req(src, dst, sent, came, peer):
        return pltpu.make_async_remote_copy(
            src_ref=src, dst_ref=dst, send_sem=sent, recv_sem=came,
            device_id=(peer, tp), device_id_type=pl.DeviceIdType.MESH,
        )

    def to_tp(src, dst, sent, came, peer):
        return pltpu.make_async_remote_copy(
            src_ref=src, dst_ref=dst, send_sem=sent, recv_sem=came,
            device_id=(me, peer), device_id_type=pl.DeviceIdType.MESH,
        )

    hold_row = holder[...].astype(F32)
    hold_col = as_column(hold_row)
    earlier = iota((moves, moves), 1) < iota((moves, moves), 0)
    rank_col = jnp.sum(jnp.where(earlier & (hold_col == hold_row), 1.0, 0.0), axis=1, keepdims=True)
    slot_col = hold_col * CAP + rank_col
    slot_row = as_row(slot_col)
    index_col = as_column(index[...].astype(F32))
    lengths = length[...].astype(F32)
    request = iota((1, reqs), 1).astype(F32)
    move_req = jnp.zeros((moves, 1), F32)
    move_live = jnp.zeros((moves, 1), F32)
    own_req = jnp.zeros((pages, 1), F32)
    own_tokens = jnp.zeros((pages, 1), F32)
    for j in range(page_slots):
        entry = table[j : j + 1, :]
        live = jnp.clip(lengths - float(j * page_len), 0.0, float(page_len))
        hit = entry == pages + iota((moves, reqs), 0)
        mine = entry == iota((pages, reqs), 0)
        move_req += jnp.sum(jnp.where(hit, request, 0.0), axis=1, keepdims=True)
        move_live += jnp.sum(jnp.where(hit, live, 0.0), axis=1, keepdims=True)
        own_req += jnp.sum(jnp.where(mine, request, 0.0), axis=1, keepdims=True)
        own_tokens += jnp.sum(jnp.where(mine, live, 0.0), axis=1, keepdims=True)
        place = jnp.sum(jnp.where(hit, slot_col, 0.0), axis=0, keepdims=True).astype(jnp.int32)
        pick_v[j : j + 1, 0:reqs] = jnp.where(entry < pages, entry, pages + place)
    own_live[...] = jnp.broadcast_to(own_tokens, own_live.shape)

    stacked = jnp.concatenate([q[:, h * head : (h + 1) * head] for h in range(heads)], axis=0)
    hr = heads * reqs

    def spread(slot_of, rows, wanted):
        lane_req = lax.rem(iota((wanted.shape[0], hr), 1), reqs).astype(F32)
        choice = jnp.where(wanted == lane_req, 1.0, 0.0).astype(BF16)
        chosen = matmul(slot_of, choice)
        same_head = lax.rem(iota((rows, hr), 0), heads) == iota((rows, hr), 1) // reqs
        return matmul(jnp.where(same_head, chosen, 0.0).astype(BF16), stacked)

    slot_rows = shards * qrows
    to_slot = ((iota((slot_rows, moves), 0) // heads).astype(F32) == slot_row).astype(F32).astype(BF16)
    slot_q = spread(to_slot, slot_rows, move_req).astype(BF16)

    request_col = as_column(adapter[...].astype(F32))
    slots = storage.shape[1]
    request_slot = jnp.sum(
        jnp.where(request_col == iota((reqs, slots), 1).astype(F32), storage[...].astype(F32), 0.0), axis=1, keepdims=True
    )
    lane = iota((moves, 128), 1).astype(F32)
    asked = jnp.where(lane == rank_col, index_col, 0.0) + jnp.where(lane == rank_col + CAP, move_live, 0.0)
    by_holder = (iota((shards, moves), 0).astype(F32) == hold_row).astype(F32).astype(BF16)
    ask = matmul(by_holder, asked.astype(BF16))
    first = iota((META, 128), 0) == 0
    upper = iota((META, 128), 1) >= 64
    for d in range(shards):
        qmsg[d, 0:qrows, :] = slot_q[d * qrows : (d + 1) * qrows]
        qmsg[d, qrows : qrows + META, :] = jnp.where(
            upper, request_slot, jnp.where(first, ask[d : d + 1, :], 0.0)
        ).astype(BF16)

    pl.semaphore_wait(barrier, shards - 1 + tps - 1)

    def ask_copy(peer, slot):
        return to_req(qmsg.at[peer], qgot.at[slot], q_sent.at[peer], q_came.at[slot], peer)

    @pl.loop(1, shards)
    def _(off):
        ask_copy(lax.rem(me + off, shards), me).start()

    qgot[pl.ds(me, 1)] = qmsg[pl.ds(me, 1)]

    own_rows = pages * heads
    to_page = ((iota((own_rows, pages), 0) // heads) == iota((own_rows, pages), 1)).astype(F32).astype(BF16)
    qown[...] = spread(to_page, own_rows, own_req).reshape(pages, heads, head)
    swap = (iota((hr, hr), 0) // heads == lax.rem(iota((hr, hr), 1), reqs)) & (
        lax.rem(iota((hr, hr), 0), heads) == iota((hr, hr), 1) // reqs
    )
    qrh[...] = matmul(swap.astype(F32).astype(BF16), stacked).reshape(reqs, heads, head)
    fresh_v[...] = fresh[...].astype(F32)
    pick_copy = pltpu.make_async_copy(pick_v, pick_s, small_sem.at[0])
    pick_copy.start()

    pool_copy.wait()
    w_copies = [
        pltpu.make_async_copy(w.at[:, pl.ds(c * columns, columns)], w_v.at[c], w_sem.at[c]) for c in range(tps)
    ]
    for copy in w_copies:
        copy.start()

    together = 4

    @pl.loop(0, pages // together)
    def _(group):
        for k in range(together):
            i = group * together + k
            top, total, part = page_partial(qown[i].astype(BF16), pool_v[i], own_live[pl.ds(i, 1), 0:1].astype(jnp.int32), head)
            o_u[i] = part
            m_u[i] = jnp.broadcast_to(top, (heads, head))
            l_u[i] = jnp.broadcast_to(total, (heads, head))

    @pl.loop(1, shards)
    def _(off):
        source = lax.rem(me + shards - off, shards)
        ask_copy(source, source).wait_recv()

    wanted = jnp.concatenate([qgot[s, qrows : qrows + META, :][0:1].astype(F32) for s in range(shards)], axis=0)
    info_v[...] = wanted.astype(jnp.int32)
    info_copy = pltpu.make_async_copy(info_v, info_s, small_sem.at[1])
    info_copy.start()
    info_copy.wait()

    block = iota((heads, 128), 1) // 32
    piece = lax.rem(iota((heads, 128), 1), 32) // 8

    def serve(source):
        queries = qgot[source, 0:qrows, :].astype(F32)
        tops = jnp.zeros((heads, 128), F32)
        totals = jnp.zeros((heads, 128), F32)
        parts = []
        for c in range(CAP):
            page = pool_v[jnp.clip(info_s[source, c], 0, pages - 1)]
            top, total, part = page_partial(
                queries[c * heads : (c + 1) * heads].astype(BF16), page, info_s[source, CAP + c], head
            )
            tops = jnp.where(block == c, top, tops)
            totals = jnp.where(block == c, total, totals)
            parts.append(part)
        high = tops.astype(BF16).astype(F32)
        rest = tops - high
        middle = rest.astype(BF16).astype(F32)
        sum_high = totals.astype(BF16).astype(F32)
        packed = jnp.where(piece == 0, high, jnp.where(piece == 1, middle, jnp.where(piece == 2, rest - middle, sum_high)))
        rmsg[source, 0:qrows, :] = jnp.concatenate(parts, axis=0).astype(BF16)
        rmsg[source, qrows : qrows + META, :] = jnp.concatenate([packed, totals - sum_high], axis=0).astype(BF16)

    def part_copy(peer, slot):
        return to_req(rmsg.at[peer], rgot.at[slot], r_sent.at[peer], r_came.at[slot], peer)

    @pl.loop(1, shards)
    def _(off):
        source = lax.rem(me + off, shards)
        serve(source)
        part_copy(source, me).start()

    serve(me)
    rgot[pl.ds(me, 1)] = rmsg[pl.ds(me, 1)]

    def unpack(source):
        parts = rgot[source, 0:qrows, :].astype(F32)
        tail = rgot[source, qrows : qrows + META, :].astype(F32)
        packed = tail[0:heads]
        tops = packed + pltpu.roll(packed, 120, 1) + pltpu.roll(packed, 112, 1)
        totals = packed + tail[heads : 2 * heads]
        for c in range(CAP):
            unit = pages + source * CAP + c
            o_u[unit] = parts[c * heads : (c + 1) * heads]
            m_u[unit] = jnp.broadcast_to(tops[:, c * 32 : c * 32 + 1], (heads, head))
            l_u[unit] = jnp.broadcast_to(totals[:, c * 32 + 24 : c * 32 + 25], (heads, head))

    unpack(me)

    @pl.loop(1, shards)
    def _(off):
        source = lax.rem(me + shards - off, shards)
        part_copy(source, source).wait_recv()
        unpack(source)

    pick_copy.wait()

    @pl.loop(0, reqs // together)
    def _(group):
        for k in range(together):
            r = group * together + k
            units = [jnp.clip(pick_s[j, r], 0, o_u.shape[0] - 1) for j in range(page_slots)]
            tops = [m_u[u] for u in units]
            new = fresh_v[pl.ds(r, 1), :]
            own = jnp.sum(qrh[r] * new[:, :head], axis=1, keepdims=True) * (1.0 / math.sqrt(head))
            overall = functools.reduce(jnp.maximum, tops)
            overall = jnp.maximum(overall, own)
            own_weight = jnp.exp(own - overall)
            above = own_weight * new[:, head:]
            below = own_weight
            for u, top in zip(units, tops):
                scale = jnp.exp(top - overall)
                above += scale * o_u[u]
                below += scale * l_u[u]
            att_f[r] = above / below

    att_b[...] = jnp.concatenate([att_f[:, h, :] for h in range(heads)], axis=1).astype(BF16)

    def att_copy(peer, slot):
        return to_req(att_b, att_all.at[slot], a_sent.at[peer], a_came.at[slot], peer)

    @pl.loop(1, shards)
    def _(off):
        att_copy(lax.rem(me + off, shards), me).start()

    att_all[pl.ds(me, 1)] = att_b[...][None]

    for copy in w_copies:
        copy.wait()

    def p_copy(peer, slot):
        return to_tp(psend.at[peer], pgot.at[slot], p_sent.at[peer], p_came.at[slot], peer)

    @pl.loop(1, tps)
    def _(off):
        peer = lax.rem(tp + off, tps)
        psend[peer] = matmul(att_b[...], w_v[peer]).astype(BF16)
        p_copy(peer, tp).start()

    total = matmul(att_b[...], w_v[tp])

    down_copy.wait()
    up_copy.wait()

    @pl.loop(1, shards)
    def _(off):
        source = lax.rem(me + shards - off, shards)
        att_copy(source, source).wait_recv()

    rows = shards * reqs
    half = rows // 2
    tags = jnp.concatenate([qgot[s, qrows : qrows + META, :] for s in range(shards)], axis=0).astype(F32)
    panel = tags[:, 64:65] - (me * panels).astype(F32)
    here = (iota((rows, panels * rank), 1) // rank).astype(F32) == panel
    low = matmul_t(att_all[...].reshape(rows, width), down_v[...])
    low = jnp.where(here, low, 0.0)
    low = low[:, :128] + low[:, 128:]
    low = low + pltpu.roll(low, 64, 1)
    left = iota((half, 128), 1) < 64
    lsend[...] = jnp.where(left, low[:half], low[half:]).astype(BF16)

    def l_copy(peer, slot):
        return to_tp(lsend, lgot.at[slot], l_sent.at[peer], l_came.at[slot], peer)

    @pl.loop(1, tps)
    def _(off):
        l_copy(lax.rem(tp + off, tps), tp).start()

    lgot[pl.ds(tp, 1)] = lsend[...][None]

    @pl.loop(1, tps)
    def _(off):
        source = lax.rem(tp + tps - off, tps)
        l_copy(source, source).wait_recv()

    whole = jnp.sum(lgot[...].astype(F32), axis=0).astype(BF16).astype(F32)
    turned = pltpu.roll(whole, 64, 1)
    both = jnp.concatenate([jnp.where(left, whole, turned), jnp.where(left, turned, whole)], axis=0)
    low_v[...] = jnp.where(here, jnp.concatenate([both, both], axis=1), 0.0).astype(BF16)

    chunk = 4 * reqs

    @pl.loop(0, rows // chunk)
    def _(c):
        term = matmul(low_v[pl.ds(pl.multiple_of(c * chunk, chunk), chunk), :], up_v[...])
        bsend[pl.ds(c * 4, 4)] = term.astype(BF16).reshape(4, reqs, columns)

    def b_copy(peer, slot):
        return to_req(bsend.at[peer], bgot.at[slot], b_sent.at[peer], b_came.at[slot], peer)

    @pl.loop(1, shards)
    def _(off):
        b_copy(lax.rem(me + off, shards), me).start()

    bgot[pl.ds(me, 1)] = bsend[pl.ds(me, 1)]

    @pl.loop(1, tps)
    def _(off):
        source = lax.rem(tp + tps - off, tps)
        p_copy(source, source).wait_recv()

    pgot[pl.ds(tp, 1)] = jnp.zeros((1, reqs, columns), BF16)
    total += jnp.sum(pgot[...].astype(F32), axis=0)

    @pl.loop(1, shards)
    def _(off):
        source = lax.rem(me + shards - off, shards)
        b_copy(source, source).wait_recv()

    total += jnp.sum(bgot[...].astype(F32), axis=0)
    out[...] = total.astype(BF16)

    @pl.loop(1, shards)
    def _(off):
        peer = lax.rem(me + off, shards)
        ask_copy(peer, me).wait_send()
        part_copy(peer, me).wait_send()
        att_copy(peer, me).wait_send()
        b_copy(peer, me).wait_send()

    @pl.loop(1, tps)
    def _(off):
        peer = lax.rem(tp + off, tps)
        p_copy(peer, tp).wait_send()
        l_copy(peer, tp).wait_send()


def local(
    shards, tps,
    queries, fresh_key_value, key_value_pool, request_page_table, cached_length, move_holder_shard, move_page_index,
    request_adapter, adapter_storage_slot, output_projection, adapter_down_panels, adapter_up_panels,
):
    reqs, width = queries.shape
    pages, page_len, _, kv = key_value_pool.shape
    head = kv // 2
    heads = width // head
    panels, _, rank = adapter_down_panels.shape
    columns = output_projection.shape[1] // tps
    qrows = CAP * heads
    units = pages + shards * CAP
    rows = shards * reqs
    dma = pltpu.SemaphoreType.DMA
    small = pl.BlockSpec(memory_space=pltpu.VMEM)
    large = pl.BlockSpec(memory_space=pl.ANY)
    return pl.pallas_call(
        functools.partial(kernel, shards, tps),
        out_shape=jax.ShapeDtypeStruct((reqs, columns), BF16),
        in_specs=[small] * 8 + [large] * 4,
        out_specs=small,
        scratch_shapes=[
            pltpu.VMEM((pages, page_len, kv), BF16),
            pltpu.VMEM((tps, width, columns), BF16),
            pltpu.VMEM((panels * rank, width), BF16),
            pltpu.VMEM((panels * rank, columns), BF16),
            pltpu.VMEM((shards, qrows + META, head), BF16),
            pltpu.VMEM((shards, qrows + META, head), BF16),
            pltpu.VMEM((shards, qrows + META, head), BF16),
            pltpu.VMEM((shards, qrows + META, head), BF16),
            pltpu.VMEM((8, 128), jnp.int32),
            pltpu.SMEM((8, 128), jnp.int32),
            pltpu.VMEM((shards, 128), jnp.int32),
            pltpu.SMEM((shards, 128), jnp.int32),
            pltpu.VMEM((pages, heads, head), F32),
            pltpu.VMEM((reqs, heads, head), F32),
            pltpu.VMEM((pages, 128), F32),
            pltpu.VMEM((reqs, kv), F32),
            pltpu.VMEM((units, heads, head), F32),
            pltpu.VMEM((units, heads, head), F32),
            pltpu.VMEM((units, heads, head), F32),
            pltpu.VMEM((reqs, heads, head), F32),
            pltpu.VMEM((reqs, width), BF16),
            pltpu.VMEM((shards, reqs, width), BF16),
            pltpu.VMEM((tps, reqs, columns), BF16),
            pltpu.VMEM((tps, reqs, columns), BF16),
            pltpu.VMEM((rows // 2, 128), BF16),
            pltpu.VMEM((tps, rows // 2, 128), BF16),
            pltpu.VMEM((rows, panels * rank), BF16),
            pltpu.VMEM((shards, reqs, columns), BF16),
            pltpu.VMEM((shards, reqs, columns), BF16),
            dma((3,)), dma((tps,)), dma((2,)),
            dma((shards,)), dma((shards,)), dma((shards,)), dma((shards,)), dma((shards,)), dma((shards,)),
            dma((tps,)), dma((tps,)), dma((tps,)), dma((tps,)),
            dma((shards,)), dma((shards,)),
        ],
        compiler_params=pltpu.CompilerParams(
            collective_id=0, has_side_effects=True, vmem_limit_bytes=48 * 1024 * 1024
        ),
    )(
        request_page_table.T,
        cached_length.reshape(1, -1),
        move_holder_shard.reshape(1, -1),
        move_page_index.reshape(1, -1),
        request_adapter.reshape(1, -1),
        adapter_storage_slot.reshape(1, -1),
        queries,
        fresh_key_value.reshape(reqs, kv),
        key_value_pool.reshape(pages, page_len, kv),
        output_projection,
        jnp.swapaxes(adapter_down_panels, 1, 2).reshape(panels * rank, width),
        adapter_up_panels.reshape(panels * rank, columns),
    )


def solution(mesh):
    shards, tps = mesh.shape["req"], mesh.shape["tp"]
    return jax.shard_map(
        functools.partial(local, shards, tps),
        mesh=mesh,
        in_specs=(
            P("req", "tp"),
            P("req", "tp", None),
            P("req", None, "tp", None),
            P("req", None),
            P("req"),
            P("req", None),
            P("req"),
            P("req"),
            P(),
            P("tp", None),
            P("req", "tp", None),
            P("req", None, "tp"),
        ),
        out_specs=P("req", "tp"),
        check_vma=False,
    )
```

time: 267 us -> 73.8 us (0.28); the launches traced: 263 us -> 73.4 us
  waiting for transfers between devices: 125 us -> 0 us
  Pallas kernels: 0 us -> 63.1 us
  blocking collectives: 46.4 us -> 0 us
  starting transfers between devices: 22.3 us -> 0 us
  matrix products: 16.3 us -> 0 us
  local copies, waits for them, and re-layouts: 24.8 us -> 10.3 us
  other arithmetic: 14.4 us -> 0 us
  between operations: 13.7 us -> 0.02 us
    all_to_all x4 -> x0, waiting for transfers between devices: 125 us -> none  [the longest x1 120 us: local(): lax.all_to_all(sent_pages, 'req', split_axis=0, concat_axis=0, tiled=True)]
    pallas_call x0 -> x1, Pallas kernels: none -> 63.1 us  [local(): pl.pallas_call(functools.partial(kernel, shards, tps), out_shape=jax.Shap...]
    psum x1 -> x0, blocking collectives: 27.7 us -> none  [local(): whole_low = lax.psum(partial_low, 'tp').astype(jnp.bfloat16)]
    gather x3 -> x0, local copies, waits for them, and re-layouts: 22.8 us -> none  [the longest x1 8.9 us: local(): extended[request_page_table]]
    all_to_all x4 -> x0, starting transfers between devices: 22.2 us -> none  [the longest x1 7.58 us: local(): lax.all_to_all(wanted, 'req', split_axis=0, concat_axis=0, tiled=True)]
    all_to_all x1 -> x0, blocking collectives: 18.7 us -> none  [local(): lax.all_to_all(correction_rows, 'req', split_axis=0, concat_axis=0, tiled...]
    dot_general x6 -> x0, matrix products: 16.3 us -> none  [the longest x1 8.9 us: local(): jnp.dot(attended, output_projection, preferred_element_type=jnp.float32)]
    unnamed x14 -> x23, local copies, waits for them, and re-layouts: 0.04 us -> 10.3 us
  transfers between devices with their start and end apart: 5 -> 0, of which waited for: 3 -> 0; matrix products, arithmetic and copies ran while one was open for 8% -> 0% of each run, Pallas kernels for 0% -> 0%
where the time goes in v1:
time: 73.8 us; the launch traced here: 73.4 us
  Pallas kernels  63.1 us (86%)
  local copies, waits for them, and re-layouts  10.3 us (14%)
    pallas_call x1, Pallas kernels, local(): pl.pallas_call(functools.partial(kernel, shards, tps), out_shape=jax.Shap...  63.1 us
    unnamed x23, local copies, waits for them, and re-layouts  10.3 us

profile of v1, /device:TPU:1, one launch (start us, length us, event | category | flops | bytes accessed | tf_op | source)
XLA Modules:
  0.0 73.4 jit_solution(4203954937837031871)
XLA Ops:
  0.0 0.0 copy-start
  0.0 2.2 %copy-done = bf16[32,256,1,256]{3,1,2,0:T(8,128)(2,1)S(1)} copy-done((bf16[32,256,1,256]{3,1,2,0:T(8,128)(2,1)S(1)}, bf16[32,256,1,256]{3,1,2,0:T(8,128)(2,1)}, u32[]{:S(2)}) %copy-start) | copy-done | bytes 4194328
  2.2 0.0 copy-start.1
  2.2 1.0 %copy-done.1 = bf16[4,1024,64]{1,2,0:T(8,128)(2,1)S(1)} copy-done((bf16[4,1024,64]{1,2,0:T(8,128)(2,1)S(1)}, bf16[4,1024,64]{1,2,0:T(8,128)(2,1)}, u32[]{:S(2)}) %copy-start.1) | copy-done | bytes 524312
  3.2 0.0 copy-start.2
  3.2 1.0 %copy-done.2 = bf16[4,64,1024]{2,1,0:T(8,128)(2,1)S(1)} copy-done((bf16[4,64,1024]{2,1,0:T(8,128)(2,1)S(1)}, bf16[4,64,1024]{2,1,0:T(8,128)(2,1)}, u32[]{:S(2)}) %copy-start.2) | copy-done | bytes 524312
  4.3 0.0 copy-start.3
  4.3 0.8 %copy-done.3 = bf16[16,1024]{1,0:T(8,128)(2,1)S(1)} copy-done((bf16[16,1024]{1,0:T(8,128)(2,1)S(1)}, bf16[16,1024]{1,0:T(8,128)(2,1)}, u32[]{:S(2)}) %copy-start.3) | copy-done | bytes 32792
  5.0 0.0 copy-start.4
  5.0 0.7 copy-done.4
  5.7 0.0 copy-start.5
  5.7 0.7 copy-done.5
  6.4 0.0 copy-start.6
  6.4 0.7 copy-done.6
  7.1 0.0 copy-start.7
  7.1 0.7 copy-done.7
  7.7 0.0 copy-start.8
  7.7 0.7 copy-done.8
  8.4 0.0 copy-start.9
  8.4 0.7 copy-done.9
  9.0 0.0 copy-start.10
  9.0 0.7 copy-done.10
  9.7 63.1 %shard_map.118 = bf16[16,1024]{1,0:T(8,128)(2,1)S(1)} custom-call(s32[4,16]{1,0:T(4,128)S(1)} %bitcast.16, s32[1,16]{1,0:T(1,128)S(1)} %bitcast.17, s32[1,32]{1,0:T(1,128)S(1)} %bitcast.18, s32[1,32]{1,0:T(1,128)S(1)} %bitcast.19, s32[1,16]{1,0:T(1,128)S(1)} %bitcast.20, s32[1,64]{1,0:T(1,128)S(1)} %bitcast.21, bf16[16,1024]{1,0:T(8,128)(2,1)S(1)} %copy-done.3, ...), custom_call_target="tpu_custom_call" | custom-call | tf_op jit(solution)/shard_map/pallas_call | solution.py:413
  72.8 0.6 copy.14
Async XLA Ops:
  0.0 2.2 %copy-start = (bf16[32,256,1,256]{3,1,2,0:T(8,128)(2,1)S(1)}, bf16[32,256,1,256]{3,1,2,0:T(8,128)(2,1)}, u32[]{:S(2)}) copy-start(bf16[32,256,1,256]{3,1,2,0:T(8,128)(2,1)} %param.14) | copy-start | bytes 12582916
  2.2 1.0 %copy-start.1 = (bf16[4,1024,64]{1,2,0:T(8,128)(2,1)S(1)}, bf16[4,1024,64]{1,2,0:T(8,128)(2,1)}, u32[]{:S(2)}) copy-start(bf16[4,1024,64]{1,2,0:T(8,128)(2,1)} %param.22) | copy-start | bytes 1572868
  3.2 1.0 %copy-start.2 = (bf16[4,64,1024]{2,1,0:T(8,128)(2,1)S(1)}, bf16[4,64,1024]{2,1,0:T(8,128)(2,1)}, u32[]{:S(2)}) copy-start(bf16[4,64,1024]{2,1,0:T(8,128)(2,1)} %param.23) | copy-start | bytes 1572868
  4.3 0.8 %copy-start.3 = (bf16[16,1024]{1,0:T(8,128)(2,1)S(1)}, bf16[16,1024]{1,0:T(8,128)(2,1)}, u32[]{:S(2)}) copy-start(bf16[16,1024]{1,0:T(8,128)(2,1)} %q.1) | copy-start | bytes 98308
  5.0 0.7 copy-start.4
  5.7 0.7 copy-start.5
  6.4 0.7 copy-start.6
  7.1 0.7 copy-start.7
  7.7 0.7 copy-start.8
  8.4 0.7 copy-start.9
  9.0 0.7 copy-start.10

commit v2 on v1

--- a/solution.py
+++ b/solution.py
@@ -37,23 +37,28 @@
     return jnp.sum(jnp.where(iota((n, n), 0) == iota((n, n), 1), column, 0.0), axis=0, keepdims=True)
 
 
-def page_partial(q, page, live, head):
-    scores = matmul_t(q, page[:, :head]) * (1.0 / math.sqrt(head))
-    there = iota(scores.shape, 1) < live
+def page_partials(queries, pages, live, head):
+    heads = queries.shape[0] // len(pages)
+    rows = [slice(k * heads, (k + 1) * heads) for k in range(len(pages))]
+    scores = [matmul_t(queries[rows[k]].astype(BF16), page[:, :head]) for k, page in enumerate(pages)]
+    scores = jnp.concatenate(scores, axis=0) * (1.0 / math.sqrt(head))
+    there = iota(scores.shape, 1).astype(F32) < live
     top = jnp.max(jnp.where(there, scores, MASKED), axis=1, keepdims=True)
-    weights = jnp.where(there, jnp.exp(scores - top), 0.0).astype(BF16)
-    total = jnp.sum(weights.astype(F32), axis=1, keepdims=True)
-    return top, total, matmul(weights, page[:, head:])
+    weights = jnp.where(there, jnp.exp(scores - top), 0.0).astype(BF16).astype(F32)
+    total = jnp.sum(weights, axis=1, keepdims=True)
+    parts = [matmul(weights[rows[k]].astype(BF16), page[:, head:]) for k, page in enumerate(pages)]
+    return top, total, jnp.concatenate(parts, axis=0)
 
 
 def kernel(
     shards, tps,
-    table, length, holder, index, adapter, storage, q, fresh, pool, w, down, up,
+    table_in, length_in, holder_in, index_in, adapter_in, storage_in, q_in, fresh_in, pool, w, down, up,
     out,
+    table, length, holder, index, adapter, storage, q, fresh,
     pool_v, w_v, down_v, up_v, qmsg, qgot, rmsg, rgot, pick_v, pick_s, info_v, info_s,
     qown, qrh, own_live, fresh_v, o_u, m_u, l_u, att_f, att_b, att_all, psend, pgot,
     lsend, lgot, low_v, bsend, bgot,
-    load_sem, w_sem, small_sem, q_sent, q_came, r_sent, r_came, a_sent, a_came,
+    in_sem, load_sem, w_sem, small_sem, q_sent, q_came, r_sent, r_came, a_sent, a_came,
     p_sent, p_came, l_sent, l_came, b_sent, b_came,
 ):
     me, tp = lax.axis_index("req"), lax.axis_index("tp")
@@ -68,6 +73,17 @@
     columns = out.shape[1]
     qrows = CAP * heads
 
+    small_copies = [
+        pltpu.make_async_copy(source, here, in_sem.at[n])
+        for n, (source, here) in enumerate(
+            (
+                (holder_in, holder), (index_in, index), (table_in, table), (length_in, length),
+                (q_in, q), (adapter_in, adapter), (storage_in, storage), (fresh_in, fresh),
+            )
+        )
+    ]
+    for copy in small_copies:
+        copy.start()
     pool_copy = pltpu.make_async_copy(pool, pool_v, load_sem.at[0])
     pool_copy.start()
     down_copy = pltpu.make_async_copy(down, down_v, load_sem.at[1])
@@ -96,6 +112,9 @@
             src_ref=src, dst_ref=dst, send_sem=sent, recv_sem=came,
             device_id=(me, peer), device_id_type=pl.DeviceIdType.MESH,
         )
+
+    for copy in small_copies:
+        copy.wait()
 
     hold_row = holder[...].astype(F32)
     hold_col = as_column(hold_row)
@@ -121,7 +140,6 @@
         own_tokens += jnp.sum(jnp.where(mine, live, 0.0), axis=1, keepdims=True)
         place = jnp.sum(jnp.where(hit, slot_col, 0.0), axis=0, keepdims=True).astype(jnp.int32)
         pick_v[j : j + 1, 0:reqs] = jnp.where(entry < pages, entry, pages + place)
-    own_live[...] = jnp.broadcast_to(own_tokens, own_live.shape)
 
     stacked = jnp.concatenate([q[:, h * head : (h + 1) * head] for h in range(heads)], axis=0)
     hr = heads * reqs
@@ -167,7 +185,8 @@
 
     own_rows = pages * heads
     to_page = ((iota((own_rows, pages), 0) // heads) == iota((own_rows, pages), 1)).astype(F32).astype(BF16)
-    qown[...] = spread(to_page, own_rows, own_req).reshape(pages, heads, head)
+    qown[...] = spread(to_page, own_rows, own_req)
+    own_live[...] = matmul(to_page, jnp.broadcast_to(own_tokens, (pages, 128)).astype(BF16))
     swap = (iota((hr, hr), 0) // heads == lax.rem(iota((hr, hr), 1), reqs)) & (
         lax.rem(iota((hr, hr), 0), heads) == iota((hr, hr), 1) // reqs
     )
@@ -183,16 +202,18 @@
     for copy in w_copies:
         copy.start()
 
-    together = 4
-
-    @pl.loop(0, pages // together)
+    batch = 16
+
+    @pl.loop(0, pages // batch)
     def _(group):
-        for k in range(together):
-            i = group * together + k
-            top, total, part = page_partial(qown[i].astype(BF16), pool_v[i], own_live[pl.ds(i, 1), 0:1].astype(jnp.int32), head)
-            o_u[i] = part
-            m_u[i] = jnp.broadcast_to(top, (heads, head))
-            l_u[i] = jnp.broadcast_to(total, (heads, head))
+        rows = pl.ds(pl.multiple_of(group * batch * heads, batch * heads), batch * heads)
+        units = pl.ds(group * batch, batch)
+        top, total, part = page_partials(
+            qown[rows, :], [pool_v.at[group * batch + k] for k in range(batch)], own_live[rows, 0:1], head
+        )
+        o_u[units] = part.reshape(batch, heads, head)
+        m_u[units] = jnp.broadcast_to(top, part.shape).reshape(batch, heads, head)
+        l_u[units] = jnp.broadcast_to(total, part.shape).reshape(batch, heads, head)
 
     @pl.loop(1, shards)
     def _(off):
@@ -208,71 +229,85 @@
     block = iota((heads, 128), 1) // 32
     piece = lax.rem(iota((heads, 128), 1), 32) // 8
 
-    def serve(source):
-        queries = qgot[source, 0:qrows, :].astype(F32)
-        tops = jnp.zeros((heads, 128), F32)
-        totals = jnp.zeros((heads, 128), F32)
-        parts = []
-        for c in range(CAP):
-            page = pool_v[jnp.clip(info_s[source, c], 0, pages - 1)]
-            top, total, part = page_partial(
-                queries[c * heads : (c + 1) * heads].astype(BF16), page, info_s[source, CAP + c], head
-            )
-            tops = jnp.where(block == c, top, tops)
-            totals = jnp.where(block == c, total, totals)
-            parts.append(part)
-        high = tops.astype(BF16).astype(F32)
-        rest = tops - high
-        middle = rest.astype(BF16).astype(F32)
-        sum_high = totals.astype(BF16).astype(F32)
-        packed = jnp.where(piece == 0, high, jnp.where(piece == 1, middle, jnp.where(piece == 2, rest - middle, sum_high)))
-        rmsg[source, 0:qrows, :] = jnp.concatenate(parts, axis=0).astype(BF16)
-        rmsg[source, qrows : qrows + META, :] = jnp.concatenate([packed, totals - sum_high], axis=0).astype(BF16)
-
     def part_copy(peer, slot):
         return to_req(rmsg.at[peer], rgot.at[slot], r_sent.at[peer], r_came.at[slot], peer)
 
-    @pl.loop(1, shards)
-    def _(off):
-        source = lax.rem(me + off, shards)
-        serve(source)
-        part_copy(source, me).start()
-
-    serve(me)
+    group_of = 4
+
+    @pl.loop(0, shards // group_of)
+    def _(group):
+        sources = [lax.rem(me + 1 + group * group_of + k, shards) for k in range(group_of)]
+        queries = jnp.concatenate([qgot[source, 0:qrows, :].astype(F32) for source in sources], axis=0)
+        picked, live = [], []
+        for source in sources:
+            for c in range(CAP):
+                picked.append(pool_v.at[jnp.clip(info_s[source, c], 0, pages - 1)])
+                live.append(jnp.full((heads, 1), info_s[source, CAP + c], jnp.int32))
+        top, total, part = page_partials(queries, picked, jnp.concatenate(live, axis=0).astype(F32), head)
+        bodies, tails = [], []
+        for k in range(group_of):
+            tops = jnp.zeros((heads, 128), F32)
+            totals = jnp.zeros((heads, 128), F32)
+            for c in range(CAP):
+                rows = slice((k * CAP + c) * heads, (k * CAP + c + 1) * heads)
+                tops = jnp.where(block == c, top[rows], tops)
+                totals = jnp.where(block == c, total[rows], totals)
+            high = tops.astype(BF16).astype(F32)
+            rest = tops - high
+            middle = rest.astype(BF16).astype(F32)
+            sum_high = totals.astype(BF16).astype(F32)
+            packed = jnp.where(
+                piece == 0, high, jnp.where(piece == 1, middle, jnp.where(piece == 2, rest - middle, sum_high))
+            )
+            bodies.append(part[k * qrows : (k + 1) * qrows].astype(BF16))
+            tails.append(jnp.concatenate([packed, totals - sum_high], axis=0).astype(BF16))
+        for source, body, tail in zip(sources, bodies, tails):
+            rmsg[source, 0:qrows, :] = body
+            rmsg[source, qrows : qrows + META, :] = tail
+        for source in sources:
+
+            @pl.when(source != me)
+            def _():
+                part_copy(source, me).start()
+
     rgot[pl.ds(me, 1)] = rmsg[pl.ds(me, 1)]
 
-    def unpack(source):
-        parts = rgot[source, 0:qrows, :].astype(F32)
-        tail = rgot[source, qrows : qrows + META, :].astype(F32)
-        packed = tail[0:heads]
-        tops = packed + pltpu.roll(packed, 120, 1) + pltpu.roll(packed, 112, 1)
-        totals = packed + tail[heads : 2 * heads]
-        for c in range(CAP):
-            unit = pages + source * CAP + c
-            o_u[unit] = parts[c * heads : (c + 1) * heads]
-            m_u[unit] = jnp.broadcast_to(tops[:, c * 32 : c * 32 + 1], (heads, head))
-            l_u[unit] = jnp.broadcast_to(totals[:, c * 32 + 24 : c * 32 + 25], (heads, head))
-
-    unpack(me)
-
-    @pl.loop(1, shards)
-    def _(off):
-        source = lax.rem(me + shards - off, shards)
-        part_copy(source, source).wait_recv()
-        unpack(source)
+    @pl.loop(0, shards // group_of)
+    def _(group):
+        sources = [lax.rem(me + 2 * shards - 1 - group * group_of - k, shards) for k in range(group_of)]
+        for source in sources:
+
+            @pl.when(source != me)
+            def _():
+                part_copy(source, source).wait_recv()
+
+        found = []
+        for source in sources:
+            part = rgot[source, 0:qrows, :].astype(F32)
+            tail = rgot[source, qrows : qrows + META, :].astype(F32)
+            packed = tail[0:heads]
+            tops = packed + pltpu.roll(packed, 120, 1) + pltpu.roll(packed, 112, 1)
+            totals = packed + tail[heads : 2 * heads]
+            top = jnp.concatenate([tops[:, c * 32 : c * 32 + 1] for c in range(CAP)], axis=0)
+            total = jnp.concatenate([totals[:, c * 32 + 24 : c * 32 + 25] for c in range(CAP)], axis=0)
+            found.append((part, jnp.broadcast_to(top, part.shape), jnp.broadcast_to(total, part.shape)))
+        for source, values in zip(sources, found):
+            units = pl.ds(pages + source * CAP, CAP)
+            for kept, value in zip((o_u, m_u, l_u), values):
+                kept[units] = value.reshape(CAP, heads, head)
 
     pick_copy.wait()
 
-    @pl.loop(0, reqs // together)
+    @pl.loop(0, reqs // group_of)
     def _(group):
-        for k in range(together):
-            r = group * together + k
+        merged = []
+        for k in range(group_of):
+            r = group * group_of + k
             units = [jnp.clip(pick_s[j, r], 0, o_u.shape[0] - 1) for j in range(page_slots)]
             tops = [m_u[u] for u in units]
             new = fresh_v[pl.ds(r, 1), :]
             own = jnp.sum(qrh[r] * new[:, :head], axis=1, keepdims=True) * (1.0 / math.sqrt(head))
-            overall = functools.reduce(jnp.maximum, tops)
-            overall = jnp.maximum(overall, own)
+            overall = jnp.maximum(functools.reduce(jnp.maximum, tops), own)
             own_weight = jnp.exp(own - overall)
             above = own_weight * new[:, head:]
             below = own_weight
@@ -280,7 +315,8 @@
                 scale = jnp.exp(top - overall)
                 above += scale * o_u[u]
                 below += scale * l_u[u]
-            att_f[r] = above / below
+            merged.append((above / below)[None])
+        att_f[pl.ds(group * group_of, group_of)] = jnp.concatenate(merged, axis=0)
 
     att_b[...] = jnp.concatenate([att_f[:, h, :] for h in range(heads)], axis=1).astype(BF16)
 
@@ -413,9 +449,17 @@
     return pl.pallas_call(
         functools.partial(kernel, shards, tps),
         out_shape=jax.ShapeDtypeStruct((reqs, columns), BF16),
-        in_specs=[small] * 8 + [large] * 4,
+        in_specs=[large] * 12,
         out_specs=small,
         scratch_shapes=[
+            pltpu.VMEM(request_page_table.shape[::-1], jnp.int32),
+            pltpu.VMEM((1, reqs), jnp.int32),
+            pltpu.VMEM((1, move_holder_shard.shape[0]), jnp.int32),
+            pltpu.VMEM((1, move_holder_shard.shape[0]), jnp.int32),
+            pltpu.VMEM((1, reqs), jnp.int32),
+            pltpu.VMEM((1, adapter_storage_slot.shape[0]), jnp.int32),
+            pltpu.VMEM((reqs, width), BF16),
+            pltpu.VMEM((reqs, kv), BF16),
             pltpu.VMEM((pages, page_len, kv), BF16),
             pltpu.VMEM((tps, width, columns), BF16),
             pltpu.VMEM((panels * rank, width), BF16),
@@ -428,9 +472,9 @@
             pltpu.SMEM((8, 128), jnp.int32),
             pltpu.VMEM((shards, 128), jnp.int32),
             pltpu.SMEM((shards, 128), jnp.int32),
-            pltpu.VMEM((pages, heads, head), F32),
+            pltpu.VMEM((pages * heads, head), F32),
             pltpu.VMEM((reqs, heads, head), F32),
-            pltpu.VMEM((pages, 128), F32),
+            pltpu.VMEM((pages * heads, 128), F32),
             pltpu.VMEM((reqs, kv), F32),
             pltpu.VMEM((units, heads, head), F32),
             pltpu.VMEM((units, heads, head), F32),
@@ -445,13 +489,13 @@
             pltpu.VMEM((rows, panels * rank), BF16),
             pltpu.VMEM((shards, reqs, columns), BF16),
             pltpu.VMEM((shards, reqs, columns), BF16),
-            dma((3,)), dma((tps,)), dma((2,)),
+            dma((8,)), dma((3,)), dma((tps,)), dma((2,)),
             dma((shards,)), dma((shards,)), dma((shards,)), dma((shards,)), dma((shards,)), dma((shards,)),
             dma((tps,)), dma((tps,)), dma((tps,)), dma((tps,)),
             dma((shards,)), dma((shards,)),
         ],
         compiler_params=pltpu.CompilerParams(
-            collective_id=0, has_side_effects=True, vmem_limit_bytes=48 * 1024 * 1024
+            collective_id=0, has_side_effects=True, vmem_limit_bytes=62 * 1024 * 1024
         ),
     )(
         request_page_table.T,

time: 73.8 us -> 47.4 us (0.64)
  Pallas kernels: 63.1 us -> 45.9 us
  local copies, waits for them, and re-layouts: 10.3 us -> 1.38 us
    pallas_call x1, Pallas kernels: 63.1 us -> 45.9 us  [local(): pl.pallas_call(functools.partial(kernel, shards, tps), out_shape=jax.Shap...]
    unnamed x23 -> x1, local copies, waits for them, and re-layouts: 10.3 us -> 1.38 us
where the time goes in v2:
time: 47.4 us; the launch traced here: 47.2 us
  Pallas kernels  45.9 us (97%)
  local copies, waits for them, and re-layouts  1.38 us (3%)
    pallas_call x1, Pallas kernels, local(): pl.pallas_call(functools.partial(kernel, shards, tps), out_shape=jax.Shap...  45.9 us
    unnamed x1, local copies, waits for them, and re-layouts  1.38 us

profile of v2, /device:TPU:1, one launch (start us, length us, event | category | flops | bytes accessed | tf_op | source)
XLA Modules:
  0.0 47.2 jit_solution(2797523344450907786)
XLA Ops:
  0.0 45.9 %shard_map.118 = bf16[16,1024]{1,0:T(8,128)(2,1)} custom-call(s32[4,16]{1,0:T(4,128)} %bitcast.16, s32[1,16]{1,0:T(1,128)} %bitcast.17, s32[1,32]{1,0:T(1,128)} %bitcast.18, s32[1,32]{1,0:T(1,128)} %bitcast.19, s32[1,16]{1,0:T(1,128)} %bitcast.20, s32[1,64]{1,0:T(1,128)} %bitcast.21, bf16[16,1024]{1,0:T(8,128)(2,1)} %q_in.1, bf16[16,256]{1,0:T(8,128)(2,1)} %bitcast.15, ...), custom_call_target="tpu_custom_call" | custom-call | tf_op jit(solution)/shard_map/pallas_call | solution.py:449
  45.9 1.4 %copy.14 = bf16[16,1024]{1,0:T(8,128)(2,1)} copy(bf16[16,1024]{1,0:T(8,128)(2,1)} %shard_map.118) | data formatting | bytes 65536

commit v3 on v2

--- a/solution.py
+++ b/solution.py
@@ -13,6 +13,7 @@
 F32 = jnp.float32
 BF16 = jnp.bfloat16
 META = 16
+GROUP = 4
 
 
 def iota(shape, dim):
@@ -57,8 +58,8 @@
     table, length, holder, index, adapter, storage, q, fresh,
     pool_v, w_v, down_v, up_v, qmsg, qgot, rmsg, rgot, pick_v, pick_s, info_v, info_s,
     qown, qrh, own_live, fresh_v, o_u, m_u, l_u, att_f, att_b, att_all, psend, pgot,
-    lsend, lgot, low_v, bsend, bgot,
-    in_sem, load_sem, w_sem, small_sem, q_sent, q_came, r_sent, r_came, a_sent, a_came,
+    lsend, lgot, bsend, bgot,
+    in_sem, load_sem, w_sem, small_sem, info_sem, q_sent, q_came, r_sent, r_came, a_sent, a_came,
     p_sent, p_came, l_sent, l_came, b_sent, b_came,
 ):
     me, tp = lax.axis_index("req"), lax.axis_index("tp")
@@ -72,6 +73,16 @@
     rank = down.shape[0] // panels
     columns = out.shape[1]
     qrows = CAP * heads
+
+    barrier = pltpu.get_barrier_semaphore()
+
+    @pl.loop(1, shards)
+    def _(off):
+        pl.semaphore_signal(barrier, inc=1, device_id=(lax.rem(me + off, shards), tp), device_id_type=pl.DeviceIdType.MESH)
+
+    @pl.loop(1, tps)
+    def _(off):
+        pl.semaphore_signal(barrier, inc=1, device_id=(me, lax.rem(tp + off, tps)), device_id_type=pl.DeviceIdType.MESH)
 
     small_copies = [
         pltpu.make_async_copy(source, here, in_sem.at[n])
@@ -91,16 +102,6 @@
     down_copy.start()
     up_copy.start()
 
-    barrier = pltpu.get_barrier_semaphore()
-
-    @pl.loop(1, shards)
-    def _(off):
-        pl.semaphore_signal(barrier, inc=1, device_id=(lax.rem(me + off, shards), tp), device_id_type=pl.DeviceIdType.MESH)
-
-    @pl.loop(1, tps)
-    def _(off):
-        pl.semaphore_signal(barrier, inc=1, device_id=(me, lax.rem(tp + off, tps)), device_id_type=pl.DeviceIdType.MESH)
-
     def to_req(src, dst, sent, came, peer):
         return pltpu.make_async_remote_copy(
             src_ref=src, dst_ref=dst, send_sem=sent, recv_sem=came,
@@ -115,6 +116,24 @@
 
     for copy in small_copies:
         copy.wait()
+
+    group_of = GROUP
+    groups = shards // group_of
+    across = group_of
+    x, y = lax.rem(me, across), me // across
+
+    def neighbours(group, way):
+        found = []
+        for k in range(group_of):
+            dx, dy = k, lax.rem(k + group + 1, groups)
+            found.append(lax.rem(y + way * dy + groups, groups) * across + lax.rem(x + way * dx + across, across))
+        return found
+
+    def before(group):
+        return neighbours(group, -1)
+
+    def after(group):
+        return neighbours(group, 1)
 
     hold_row = holder[...].astype(F32)
     hold_col = as_column(hold_row)
@@ -177,9 +196,10 @@
     def ask_copy(peer, slot):
         return to_req(qmsg.at[peer], qgot.at[slot], q_sent.at[peer], q_came.at[slot], peer)
 
-    @pl.loop(1, shards)
-    def _(off):
-        ask_copy(lax.rem(me + off, shards), me).start()
+    for group in range(groups):
+        for k, peer in enumerate(after(group)):
+            if not (group == groups - 1 and k == 0):
+                ask_copy(peer, me).start()
 
     qgot[pl.ds(me, 1)] = qmsg[pl.ds(me, 1)]
 
@@ -215,16 +235,22 @@
         m_u[units] = jnp.broadcast_to(top, part.shape).reshape(batch, heads, head)
         l_u[units] = jnp.broadcast_to(total, part.shape).reshape(batch, heads, head)
 
-    @pl.loop(1, shards)
-    def _(off):
-        source = lax.rem(me + shards - off, shards)
-        ask_copy(source, source).wait_recv()
-
-    wanted = jnp.concatenate([qgot[s, qrows : qrows + META, :][0:1].astype(F32) for s in range(shards)], axis=0)
-    info_v[...] = wanted.astype(jnp.int32)
-    info_copy = pltpu.make_async_copy(info_v, info_s, small_sem.at[1])
-    info_copy.start()
-    info_copy.wait()
+    def info_copy(group):
+        return pltpu.make_async_copy(info_v.at[group], info_s.at[group], info_sem.at[group])
+
+    def prepare(group):
+        sources = before(group)
+        for source in sources:
+
+            @pl.when(source != me)
+            def _():
+                ask_copy(source, source).wait_recv()
+
+        wanted = [qgot[source, qrows : qrows + META, :][0:1].astype(F32) for source in sources]
+        info_v[group] = jnp.concatenate(wanted + wanted, axis=0).astype(jnp.int32)
+        info_copy(group).start()
+
+    prepare(0)
 
     block = iota((heads, 128), 1) // 32
     piece = lax.rem(iota((heads, 128), 1), 32) // 8
@@ -232,17 +258,20 @@
     def part_copy(peer, slot):
         return to_req(rmsg.at[peer], rgot.at[slot], r_sent.at[peer], r_came.at[slot], peer)
 
-    group_of = 4
-
-    @pl.loop(0, shards // group_of)
+    @pl.loop(0, groups)
     def _(group):
-        sources = [lax.rem(me + 1 + group * group_of + k, shards) for k in range(group_of)]
+        @pl.when(group + 1 < groups)
+        def _():
+            prepare(group + 1)
+
+        info_copy(group).wait()
+        sources = before(group)
         queries = jnp.concatenate([qgot[source, 0:qrows, :].astype(F32) for source in sources], axis=0)
         picked, live = [], []
-        for source in sources:
+        for k in range(group_of):
             for c in range(CAP):
-                picked.append(pool_v.at[jnp.clip(info_s[source, c], 0, pages - 1)])
-                live.append(jnp.full((heads, 1), info_s[source, CAP + c], jnp.int32))
+                picked.append(pool_v.at[jnp.clip(info_s[group, k, c], 0, pages - 1)])
+                live.append(jnp.full((heads, 1), info_s[group, k, CAP + c], jnp.int32))
         top, total, part = page_partials(queries, picked, jnp.concatenate(live, axis=0).astype(F32), head)
         bodies, tails = [], []
         for k in range(group_of):
@@ -272,9 +301,9 @@
 
     rgot[pl.ds(me, 1)] = rmsg[pl.ds(me, 1)]
 
-    @pl.loop(0, shards // group_of)
+    @pl.loop(0, groups)
     def _(group):
-        sources = [lax.rem(me + 2 * shards - 1 - group * group_of - k, shards) for k in range(group_of)]
+        sources = after(group)
         for source in sources:
 
             @pl.when(source != me)
@@ -323,10 +352,6 @@
     def att_copy(peer, slot):
         return to_req(att_b, att_all.at[slot], a_sent.at[peer], a_came.at[slot], peer)
 
-    @pl.loop(1, shards)
-    def _(off):
-        att_copy(lax.rem(me + off, shards), me).start()
-
     att_all[pl.ds(me, 1)] = att_b[...][None]
 
     for copy in w_copies:
@@ -335,98 +360,121 @@
     def p_copy(peer, slot):
         return to_tp(psend.at[peer], pgot.at[slot], p_sent.at[peer], p_came.at[slot], peer)
 
-    @pl.loop(1, tps)
-    def _(off):
-        peer = lax.rem(tp + off, tps)
+    def project(step):
+        peer = lax.rem(tp + step, tps)
         psend[peer] = matmul(att_b[...], w_v[peer]).astype(BF16)
         p_copy(peer, tp).start()
 
+    steps = [list(range(1, tps))[group::groups] for group in range(groups)]
+    for group in range(groups):
+        peers = after(group)[1 if group == groups - 1 else 0 :]
+        for peer in peers:
+            att_copy(peer, me).start()
+
+    for step in range(1, tps):
+        project(step)
     total = matmul(att_b[...], w_v[tp])
 
     down_copy.wait()
     up_copy.wait()
 
-    @pl.loop(1, shards)
-    def _(off):
-        source = lax.rem(me + shards - off, shards)
-        att_copy(source, source).wait_recv()
-
-    rows = shards * reqs
-    half = rows // 2
-    tags = jnp.concatenate([qgot[s, qrows : qrows + META, :] for s in range(shards)], axis=0).astype(F32)
-    panel = tags[:, 64:65] - (me * panels).astype(F32)
-    here = (iota((rows, panels * rank), 1) // rank).astype(F32) == panel
-    low = matmul_t(att_all[...].reshape(rows, width), down_v[...])
-    low = jnp.where(here, low, 0.0)
-    low = low[:, :128] + low[:, 128:]
-    low = low + pltpu.roll(low, 64, 1)
+    many = group_of * reqs
+    half = many // 2
     left = iota((half, 128), 1) < 64
-    lsend[...] = jnp.where(left, low[:half], low[half:]).astype(BF16)
-
-    def l_copy(peer, slot):
-        return to_tp(lsend, lgot.at[slot], l_sent.at[peer], l_came.at[slot], peer)
-
-    @pl.loop(1, tps)
-    def _(off):
-        l_copy(lax.rem(tp + off, tps), tp).start()
-
-    lgot[pl.ds(tp, 1)] = lsend[...][None]
-
-    @pl.loop(1, tps)
-    def _(off):
-        source = lax.rem(tp + tps - off, tps)
-        l_copy(source, source).wait_recv()
-
-    whole = jnp.sum(lgot[...].astype(F32), axis=0).astype(BF16).astype(F32)
-    turned = pltpu.roll(whole, 64, 1)
-    both = jnp.concatenate([jnp.where(left, whole, turned), jnp.where(left, turned, whole)], axis=0)
-    low_v[...] = jnp.where(here, jnp.concatenate([both, both], axis=1), 0.0).astype(BF16)
-
-    chunk = 4 * reqs
-
-    @pl.loop(0, rows // chunk)
-    def _(c):
-        term = matmul(low_v[pl.ds(pl.multiple_of(c * chunk, chunk), chunk), :], up_v[...])
-        bsend[pl.ds(c * 4, 4)] = term.astype(BF16).reshape(4, reqs, columns)
+    panel_of = (iota((many, panels * rank), 1) // rank + me * panels).astype(F32)
+
+    def l_copy(group, peer, slot):
+        return to_tp(lsend.at[group], lgot.at[group, slot], l_sent.at[group, peer], l_came.at[group, slot], peer)
 
     def b_copy(peer, slot):
         return to_req(bsend.at[peer], bgot.at[slot], b_sent.at[peer], b_came.at[slot], peer)
 
-    @pl.loop(1, shards)
-    def _(off):
-        b_copy(lax.rem(me + off, shards), me).start()
-
-    bgot[pl.ds(me, 1)] = bsend[pl.ds(me, 1)]
-
-    @pl.loop(1, tps)
-    def _(off):
-        source = lax.rem(tp + tps - off, tps)
-        p_copy(source, source).wait_recv()
-
-    pgot[pl.ds(tp, 1)] = jnp.zeros((1, reqs, columns), BF16)
-    total += jnp.sum(pgot[...].astype(F32), axis=0)
-
-    @pl.loop(1, shards)
-    def _(off):
-        source = lax.rem(me + shards - off, shards)
-        b_copy(source, source).wait_recv()
-
-    total += jnp.sum(bgot[...].astype(F32), axis=0)
-    out[...] = total.astype(BF16)
+    def stored_here(sources):
+        tags = jnp.concatenate([qgot[source, qrows : qrows + META, :] for source in sources], axis=0).astype(F32)
+        return panel_of == tags[:, 64:65]
+
+    def go_down(group):
+        sources = before(group)
+        for source in sources:
+
+            @pl.when(source != me)
+            def _():
+                att_copy(source, source).wait_recv()
+
+        low = matmul_t(jnp.concatenate([att_all[source] for source in sources], axis=0), down_v[...])
+        low = jnp.where(stored_here(sources), low, 0.0)
+        low = low[:, :128] + low[:, 128:]
+        low = low + pltpu.roll(low, 64, 1)
+        low = jnp.where(left, low[:half], low[half:]).astype(BF16)
+        lsend[group] = low
+        lgot[group, pl.ds(tp, 1)] = low[None]
+
+        @pl.loop(1, tps)
+        def _(off):
+            l_copy(group, lax.rem(tp + off, tps), tp).start()
+
+    def go_up(group):
+        sources = before(group)
+
+        @pl.loop(1, tps)
+        def _(off):
+            source = lax.rem(tp + tps - off, tps)
+            l_copy(group, source, source).wait_recv()
+
+        whole = jnp.sum(lgot[group].astype(F32), axis=0).astype(BF16).astype(F32)
+        turned = pltpu.roll(whole, 64, 1)
+        both = jnp.concatenate([jnp.where(left, whole, turned), jnp.where(left, turned, whole)], axis=0)
+        both = jnp.where(stored_here(sources), jnp.concatenate([both, both], axis=1), 0.0).astype(BF16)
+        term = matmul(both, up_v[...]).astype(BF16)
+        for k, source in enumerate(sources):
+            bsend[source] = term[k * reqs : (k + 1) * reqs]
+        for source in sources:
+
+            @pl.when(source != me)
+            def _():
+                b_copy(source, me).start()
 
     @pl.loop(1, shards)
     def _(off):
         peer = lax.rem(me + off, shards)
         ask_copy(peer, me).wait_send()
         part_copy(peer, me).wait_send()
-        att_copy(peer, me).wait_send()
-        b_copy(peer, me).wait_send()
+
+    ahead = 3
+    for group in range(groups + ahead):
+        if group < groups:
+            go_down(group)
+        if group >= ahead - 1 and group - ahead + 1 < groups:
+            go_up(group - ahead + 1)
+
+    @pl.loop(1, shards)
+    def _(off):
+        att_copy(lax.rem(me + off, shards), me).wait_send()
 
     @pl.loop(1, tps)
     def _(off):
         peer = lax.rem(tp + off, tps)
         p_copy(peer, tp).wait_send()
-        l_copy(peer, tp).wait_send()
+        for group in range(groups):
+            l_copy(group, peer, tp).wait_send()
+
+    def add_projected(off, total):
+        source = lax.rem(tp + tps - off, tps)
+        p_copy(source, source).wait_recv()
+        return total + pgot[source].astype(F32)
+
+    total = lax.fori_loop(1, tps, add_projected, total)
+
+    total += bsend[me].astype(F32)
+    for group in range(groups):
+        others = slice(1 if group == groups - 1 else 0, group_of)
+        for source in after(group)[others]:
+            b_copy(source, source).wait_recv()
+            total += bgot[source].astype(F32)
+        if group == groups - 1:
+            out[...] = total.astype(BF16)
+        for peer in before(group)[others]:
+            b_copy(peer, me).wait_send()
 
 
 def local(
@@ -442,7 +490,7 @@
     columns = output_projection.shape[1] // tps
     qrows = CAP * heads
     units = pages + shards * CAP
-    rows = shards * reqs
+    groups = shards // GROUP
     dma = pltpu.SemaphoreType.DMA
     small = pl.BlockSpec(memory_space=pltpu.VMEM)
     large = pl.BlockSpec(memory_space=pl.ANY)
@@ -470,8 +518,8 @@
             pltpu.VMEM((shards, qrows + META, head), BF16),
             pltpu.VMEM((8, 128), jnp.int32),
             pltpu.SMEM((8, 128), jnp.int32),
-            pltpu.VMEM((shards, 128), jnp.int32),
-            pltpu.SMEM((shards, 128), jnp.int32),
+            pltpu.VMEM((groups, 2 * GROUP, 128), jnp.int32),
+            pltpu.SMEM((groups, 2 * GROUP, 128), jnp.int32),
             pltpu.VMEM((pages * heads, head), F32),
             pltpu.VMEM((reqs, heads, head), F32),
             pltpu.VMEM((pages * heads, 128), F32),
@@ -484,20 +532,19 @@
             pltpu.VMEM((shards, reqs, width), BF16),
             pltpu.VMEM((tps, reqs, columns), BF16),
             pltpu.VMEM((tps, reqs, columns), BF16),
-            pltpu.VMEM((rows // 2, 128), BF16),
-            pltpu.VMEM((tps, rows // 2, 128), BF16),
-            pltpu.VMEM((rows, panels * rank), BF16),
+            pltpu.VMEM((groups, GROUP * reqs // 2, 128), BF16),
+            pltpu.VMEM((groups, tps, GROUP * reqs // 2, 128), BF16),
             pltpu.VMEM((shards, reqs, columns), BF16),
             pltpu.VMEM((shards, reqs, columns), BF16),
-            dma((8,)), dma((3,)), dma((tps,)), dma((2,)),
+            dma((8,)), dma((3,)), dma((tps,)), dma((1,)), dma((groups,)),
             dma((shards,)), dma((shards,)), dma((shards,)), dma((shards,)), dma((shards,)), dma((shards,)),
-            dma((tps,)), dma((tps,)), dma((tps,)), dma((tps,)),
+            dma((tps,)), dma((tps,)), dma((groups, tps)), dma((groups, tps)),
             dma((shards,)), dma((shards,)),
         ],
         compiler_params=pltpu.CompilerParams(
-            collective_id=0, has_side_effects=True, vmem_limit_bytes=62 * 1024 * 1024
+            collective_id=0, has_side_effects=True, vmem_limit_bytes=48 * 1024 * 1024
         ),
-    )(
+    )(*(pltpu.with_memory_space_constraint(operand, pltpu.HBM) for operand in (
         request_page_table.T,
         cached_length.reshape(1, -1),
         move_holder_shard.reshape(1, -1),
@@ -510,7 +557,7 @@
         output_projection,
         jnp.swapaxes(adapter_down_panels, 1, 2).reshape(panels * rank, width),
         adapter_up_panels.reshape(panels * rank, columns),
-    )
+    )))
 
 
 def solution(mesh):

time: 47.4 us -> 42.8 us (0.903)
  Pallas kernels: 45.9 us -> 42.1 us
  local copies, waits for them, and re-layouts: 1.38 us -> 0.62 us
    pallas_call x1, Pallas kernels: 45.9 us -> 42.1 us  [local(): pl.pallas_call(functools.partial(kernel, shards, tps), out_shape=jax.Shap...]
    unnamed x1, local copies, waits for them, and re-layouts: 1.38 us -> 0.62 us
where the time goes in v3:
time: 42.8 us; the launch traced here: 42.7 us
  Pallas kernels  42.1 us (98%)
  local copies, waits for them, and re-layouts  0.62 us (1%)
    pallas_call x1, Pallas kernels, local(): pl.pallas_call(functools.partial(kernel, shards, tps), out_shape=jax.Shap...  42.1 us

profile of v3, /device:TPU:1, one launch (start us, length us, event | category | flops | bytes accessed | tf_op | source)
XLA Modules:
  0.0 42.7 jit_solution(18425958814926376340)
XLA Ops:
  0.0 42.1 %shard_map.118 = bf16[16,1024]{1,0:T(8,128)(2,1)S(1)} custom-call(s32[4,16]{1,0:T(4,128)} %bitcast.16, s32[1,16]{1,0:T(1,128)} %bitcast.17, s32[1,32]{1,0:T(1,128)} %bitcast.18, s32[1,32]{1,0:T(1,128)} %bitcast.19, s32[1,16]{1,0:T(1,128)} %bitcast.20, s32[1,64]{1,0:T(1,128)} %bitcast.21, bf16[16,1024]{1,0:T(8,128)(2,1)} %q_in.1, bf16[16,256]{1,0:T(8,128)(2,1)} %bitcast.15, ...), custom_call_target="tpu_custom_call" | custom-call | tf_op jit(solution)/shard_map/pallas_call | solution.py:497
  42.1 0.6 %copy.14 = bf16[16,1024]{1,0:T(8,128)(2,1)} copy(bf16[16,1024]{1,0:T(8,128)(2,1)S(1)} %shard_map.118) | data formatting | bytes 65536

commit v4 on v3

--- a/solution.py
+++ b/solution.py
@@ -327,11 +327,10 @@
 
     pick_copy.wait()
 
-    @pl.loop(0, reqs // group_of)
-    def _(group):
+    @pl.loop(0, 1)
+    def _(_):
         merged = []
-        for k in range(group_of):
-            r = group * group_of + k
+        for r in range(reqs):
             units = [jnp.clip(pick_s[j, r], 0, o_u.shape[0] - 1) for j in range(page_slots)]
             tops = [m_u[u] for u in units]
             new = fresh_v[pl.ds(r, 1), :]
@@ -345,7 +344,7 @@
                 above += scale * o_u[u]
                 below += scale * l_u[u]
             merged.append((above / below)[None])
-        att_f[pl.ds(group * group_of, group_of)] = jnp.concatenate(merged, axis=0)
+        att_f[...] = jnp.concatenate(merged, axis=0)
 
     att_b[...] = jnp.concatenate([att_f[:, h, :] for h in range(heads)], axis=1).astype(BF16)
 

time: 42.8 us -> 42.6 us (level)
  no operation moved by 1% of the time
where the time goes in v4:
time: 42.6 us; the launch traced here: 42.5 us
  Pallas kernels  41.9 us (98%)
  local copies, waits for them, and re-layouts  0.62 us (1%)
    pallas_call x1, Pallas kernels, local(): pl.pallas_call(functools.partial(kernel, shards, tps), out_shape=jax.Shap...  41.9 us

profile of v4, /device:TPU:1, one launch (start us, length us, event | category | flops | bytes accessed | tf_op | source)
XLA Modules:
  0.0 42.5 jit_solution(10168946237624041310)
XLA Ops:
  0.0 41.9 %shard_map.118 = bf16[16,1024]{1,0:T(8,128)(2,1)S(1)} custom-call(s32[4,16]{1,0:T(4,128)} %bitcast.16, s32[1,16]{1,0:T(1,128)} %bitcast.17, s32[1,32]{1,0:T(1,128)} %bitcast.18, s32[1,32]{1,0:T(1,128)} %bitcast.19, s32[1,16]{1,0:T(1,128)} %bitcast.20, s32[1,64]{1,0:T(1,128)} %bitcast.21, bf16[16,1024]{1,0:T(8,128)(2,1)} %q_in.1, bf16[16,256]{1,0:T(8,128)(2,1)} %bitcast.15, ...), custom_call_target="tpu_custom_call" | custom-call | tf_op jit(solution)/shard_map/pallas_call | solution.py:496
  41.9 0.6 %copy.14 = bf16[16,1024]{1,0:T(8,128)(2,1)} copy(bf16[16,1024]{1,0:T(8,128)(2,1)S(1)} %shard_map.118) | data formatting | bytes 65536

commit v5 on v4

--- a/solution.py
+++ b/solution.py
@@ -56,7 +56,7 @@
     table_in, length_in, holder_in, index_in, adapter_in, storage_in, q_in, fresh_in, pool, w, down, up,
     out,
     table, length, holder, index, adapter, storage, q, fresh,
-    pool_v, w_v, down_v, up_v, qmsg, qgot, rmsg, rgot, pick_v, pick_s, info_v, info_s,
+    pool_v, w_v, down_v, down_t, here_v, up_v, qmsg, qgot, rmsg, rgot, pick_v, pick_s, info_v, info_s,
     qown, qrh, own_live, fresh_v, o_u, m_u, l_u, att_f, att_b, att_all, psend, pgot,
     lsend, lgot, bsend, bgot,
     in_sem, load_sem, w_sem, small_sem, info_sem, q_sent, q_came, r_sent, r_came, a_sent, a_came,
@@ -249,6 +249,9 @@
         wanted = [qgot[source, qrows : qrows + META, :][0:1].astype(F32) for source in sources]
         info_v[group] = jnp.concatenate(wanted + wanted, axis=0).astype(jnp.int32)
         info_copy(group).start()
+
+    down_copy.wait()
+    down_t[...] = down_v[...].T
 
     prepare(0)
 
@@ -374,7 +377,6 @@
         project(step)
     total = matmul(att_b[...], w_v[tp])
 
-    down_copy.wait()
     up_copy.wait()
 
     many = group_of * reqs
@@ -400,8 +402,7 @@
             def _():
                 att_copy(source, source).wait_recv()
 
-        low = matmul_t(jnp.concatenate([att_all[source] for source in sources], axis=0), down_v[...])
-        low = jnp.where(stored_here(sources), low, 0.0)
+        low = matmul(jnp.concatenate([att_all[source] for source in sources], axis=0), down_t[...]) * here_v[group]
         low = low[:, :128] + low[:, 128:]
         low = low + pltpu.roll(low, 64, 1)
         low = jnp.where(left, low[:half], low[half:]).astype(BF16)
@@ -423,7 +424,7 @@
         whole = jnp.sum(lgot[group].astype(F32), axis=0).astype(BF16).astype(F32)
         turned = pltpu.roll(whole, 64, 1)
         both = jnp.concatenate([jnp.where(left, whole, turned), jnp.where(left, turned, whole)], axis=0)
-        both = jnp.where(stored_here(sources), jnp.concatenate([both, both], axis=1), 0.0).astype(BF16)
+        both = (jnp.concatenate([both, both], axis=1) * here_v[group]).astype(BF16)
         term = matmul(both, up_v[...]).astype(BF16)
         for k, source in enumerate(sources):
             bsend[source] = term[k * reqs : (k + 1) * reqs]
@@ -439,6 +440,8 @@
         ask_copy(peer, me).wait_send()
         part_copy(peer, me).wait_send()
 
+    for group in range(groups):
+        here_v[group] = stored_here(before(group)).astype(F32)
     ahead = 3
     for group in range(groups + ahead):
         if group < groups:
@@ -510,6 +513,8 @@
             pltpu.VMEM((pages, page_len, kv), BF16),
             pltpu.VMEM((tps, width, columns), BF16),
             pltpu.VMEM((panels * rank, width), BF16),
+            pltpu.VMEM((width, panels * rank), BF16),
+            pltpu.VMEM((groups, GROUP * reqs, panels * rank), F32),
             pltpu.VMEM((panels * rank, columns), BF16),
             pltpu.VMEM((shards, qrows + META, head), BF16),
             pltpu.VMEM((shards, qrows + META, head), BF16),

time: 42.6 us -> 43.1 us (1.012)
  Pallas kernels: 41.9 us -> 42.4 us
    pallas_call x1, Pallas kernels: 41.9 us -> 42.4 us  [local(): pl.pallas_call(functools.partial(kernel, shards, tps), out_shape=jax.Shap...]
where the time goes in v5:
time: 43.1 us
  Pallas kernels  42.4 us (98%)
  local copies, waits for them, and re-layouts  0.62 us (1%)
    pallas_call x1, Pallas kernels, local(): pl.pallas_call(functools.partial(kernel, shards, tps), out_shape=jax.Shap...  42.4 us

profile of v5, /device:TPU:1, one launch (start us, length us, event | category | flops | bytes accessed | tf_op | source)
XLA Modules:
  0.0 43.1 jit_solution(6278350002033510520)
XLA Ops:
  0.0 42.4 %shard_map.118 = bf16[16,1024]{1,0:T(8,128)(2,1)S(1)} custom-call(s32[4,16]{1,0:T(4,128)} %bitcast.16, s32[1,16]{1,0:T(1,128)} %bitcast.17, s32[1,32]{1,0:T(1,128)} %bitcast.18, s32[1,32]{1,0:T(1,128)} %bitcast.19, s32[1,16]{1,0:T(1,128)} %bitcast.20, s32[1,64]{1,0:T(1,128)} %bitcast.21, bf16[16,1024]{1,0:T(8,128)(2,1)} %q_in.1, bf16[16,256]{1,0:T(8,128)(2,1)} %bitcast.15, ...), custom_call_target="tpu_custom_call" | custom-call | tf_op jit(solution)/shard_map/pallas_call | solution.py:499
  42.4 0.6 %copy.14 = bf16[16,1024]{1,0:T(8,128)(2,1)} copy(bf16[16,1024]{1,0:T(8,128)(2,1)S(1)} %shard_map.118) | data formatting | bytes 65536

commit v6 on v4

--- a/solution.py
+++ b/solution.py
@@ -362,7 +362,6 @@
     def project(step):
         peer = lax.rem(tp + step, tps)
         psend[peer] = matmul(att_b[...], w_v[peer]).astype(BF16)
-        p_copy(peer, tp).start()
 
     steps = [list(range(1, tps))[group::groups] for group in range(groups)]
     for group in range(groups):
@@ -443,6 +442,11 @@
     for group in range(groups + ahead):
         if group < groups:
             go_down(group)
+        if group == 3:
+            @pl.loop(1, tps)
+            def _(off):
+                p_copy(lax.rem(tp + off, tps), tp).start()
+
         if group >= ahead - 1 and group - ahead + 1 < groups:
             go_up(group - ahead + 1)
 

time: 42.6 us -> 42.5 us (level)
  no operation moved by 1% of the time
where the time goes in v6:
time: 42.5 us
  Pallas kernels  41.8 us (98%)
  local copies, waits for them, and re-layouts  0.62 us (1%)
    pallas_call x1, Pallas kernels, local(): pl.pallas_call(functools.partial(kernel, shards, tps), out_shape=jax.Shap...  41.8 us

profile of v6, /device:TPU:1, one launch (start us, length us, event | category | flops | bytes accessed | tf_op | source)
XLA Modules:
  0.0 42.5 jit_solution(5580003560671928114)
XLA Ops:
  0.0 41.8 %shard_map.118 = bf16[16,1024]{1,0:T(8,128)(2,1)S(1)} custom-call(s32[4,16]{1,0:T(4,128)} %bitcast.16, s32[1,16]{1,0:T(1,128)} %bitcast.17, s32[1,32]{1,0:T(1,128)} %bitcast.18, s32[1,32]{1,0:T(1,128)} %bitcast.19, s32[1,16]{1,0:T(1,128)} %bitcast.20, s32[1,64]{1,0:T(1,128)} %bitcast.21, bf16[16,1024]{1,0:T(8,128)(2,1)} %q_in.1, bf16[16,256]{1,0:T(8,128)(2,1)} %bitcast.15, ...), custom_call_target="tpu_custom_call" | custom-call | tf_op jit(solution)/shard_map/pallas_call | solution.py:500
  41.8 0.6 %copy.14 = bf16[16,1024]{1,0:T(8,128)(2,1)} copy(bf16[16,1024]{1,0:T(8,128)(2,1)S(1)} %shard_map.118) | data formatting | bytes 65536
